TPU v7x, 32 devices: a whole 2x2x4 slice. The times are simulated.
32 devices in a mesh: pipe: 4 (over y, x), expert: 8 (over z, core).
Axes of the slice: x: 2, y: 2, z: 4, core: 2. Of those that a mesh axis runs over, the one named last changes fastest.
Arguments:
- out_grad: bfloat16 [4, 1, 1024, 1024], P('pipe', None, 'expert'), may hold values from -6 to 6
- gate_weights: float32 [4, 1, 1024, 8], P('pipe', None, 'expert'), may hold values from 0.05 to 1
- routes: int32 [4, 1, 1024, 8], P('pipe', None, 'expert'), may hold values from 0 to 7, as said below
- hidden_act: bfloat16 [4, 1, 8, 1024, 512], P('pipe', None, 'expert'), may hold values from -0.59765625 to 0.59765625
- down_weight: bfloat16 [4, 8, 256, 1024], P('pipe', 'expert'), may hold values from -0.1875 to 0.1875
- block_scales: float32 [4, 8, 2, 8], P('pipe', 'expert'), may hold values from 0.25 to 4
Outputs:
- hidden_grad: bfloat16 [4, 1, 8, 1024, 512], P('pipe', None, 'expert')
- weight_grad: bfloat16 [4, 8, 256, 1024], P('pipe', 'expert')
Inputs may be any that keep to these rules, and one draw needn't show every extreme that they name: `routes`: each token names 8 different experts. Within one section and one micro-batch, the 128 tokens of each aligned block name every expert exactly 128 times.
All inputs are finite; a program needn't handle non-finite values.
Results may differ from a plain program's by a relative error of at most 0.0075.
Values may be sent and summed in bfloat16 or wider, within the bound.
A program may use at most 64 MiB of HBM per device.

v0:
```python
import jax
import jax.numpy as jnp
from jax import lax
from jax.sharding import PartitionSpec as P

D = 1024
QBLOCK = 128


def partner(block, axis, distance):
    count = lax.axis_size(axis)
    route = []
    for low in range(count):
        high = low | 1 << distance
        if high != low and high < count:
            route += [(low, high), (high, low)]
    return lax.ppermute(block, axis, route)


def expand(scales):
    return jnp.repeat(jnp.repeat(scales, QBLOCK, axis=0), QBLOCK, axis=1)


def on_device(out_grad, gate_weights, routes, hidden_act, down_weight, block_scales):
    experts = lax.axis_size("expert")
    gradient = out_grad[0]
    gate_rows = gate_weights[0]
    route_rows = routes[0]
    tok_count = gradient.shape[1]
    top_count = route_rows.shape[2]
    capacity = tok_count * top_count // experts
    dequant_half = (down_weight[0, 0].astype(jnp.float32) * expand(block_scales[0, 0])).astype(
        jnp.bfloat16
    )
    activations = hidden_act[0, :, 0]
    scaled = (gate_rows[0][:, :, None] * gradient[0][:, None, :].astype(jnp.float32)).astype(
        jnp.bfloat16
    )
    scaled = scaled.reshape(tok_count * top_count, D)
    expert_ids = route_rows[0].reshape(-1)
    onehot = (expert_ids[:, None] == jnp.arange(experts, dtype=jnp.int32)[None, :]).astype(
        jnp.int32
    )
    before = jnp.cumsum(onehot, axis=0) - onehot
    slot_rank = jnp.sum(before * onehot, axis=1)
    slot_index = expert_ids * capacity + slot_rank
    filled = jnp.zeros((experts * capacity, D), jnp.bfloat16).at[slot_index].set(scaled)
    received = [
        lax.all_to_all(
            filled.reshape(experts, capacity, D), "expert", split_axis=0, concat_axis=0, tiled=True
        ).reshape(-1, D)
    ]
    rows_stack = jnp.stack(received)
    sections = lax.axis_size("pipe")
    half_size = sections // 2
    pair_bit = sections.bit_length() - 2
    upper_half = (lax.axis_index("pipe") >= half_size).astype(jnp.int32)
    is_upper = upper_half == 1
    half_rows = dequant_half.shape[0]
    both_dims = (((0, 1), (0, 1)), ((), ()))
    row_dims = (((2,), (1,)), ((), ()))
    other_half = partner(dequant_half, "pipe", pair_bit)
    whole = jnp.where(
        is_upper,
        jnp.concatenate([other_half, dequant_half], axis=0),
        jnp.concatenate([dequant_half, other_half], axis=0),
    )
    hidden = lax.dot_general(
        rows_stack, whole, row_dims, preferred_element_type=jnp.float32
    ).astype(jnp.bfloat16)
    section_sum = lax.dot_general(
        activations, rows_stack, both_dims, preferred_element_type=jnp.float32
    )
    their_part = lax.dynamic_slice_in_dim(
        section_sum, (1 - upper_half) * half_rows, half_rows, 0
    ).astype(jnp.bfloat16)
    received_part = partner(their_part, "pipe", pair_bit)
    own_part = lax.dynamic_slice_in_dim(section_sum, upper_half * half_rows, half_rows, 0)
    rounded = lax.optimization_barrier(own_part.astype(jnp.bfloat16)).astype(jnp.float32)
    weight_grad = (rounded + received_part.astype(jnp.float32)).astype(jnp.bfloat16)
    hidden_grad = hidden[None, :, None]
    return (hidden_grad, weight_grad[None, None])


def solution(mesh):
    in_specs = (
        P("pipe", None, "expert", None),
        P("pipe", None, "expert", None),
        P("pipe", None, "expert", None),
        P("pipe", None, "expert", None, None),
        P("pipe", "expert", None, None),
        P("pipe", "expert", None, None),
    )
    out_specs = (P("pipe", None, "expert", None, None), P("pipe", "expert", None, None))
    return jax.shard_map(
        on_device, mesh=mesh, in_specs=in_specs, out_specs=out_specs, check_vma=False
    )
```

profile of v0, /device:TPU:0, one launch (start us, length us, event | category | flops | bytes accessed | tf_op | source)
XLA Modules:
  0.0 88.4 jit_solution(5513799619677181903)
XLA Ops:
  0.6 0.0 copy-start
  0.6 0.8 broadcast_multiply_fusion
  1.4 0.8 copy.10
  2.2 0.1 eq.32
  2.3 0.1 eq.28
  2.4 0.1 copy.9
  2.5 0.1 mul.48
  2.6 2.3 %reduce-window.6 = s32[8,8,128]{2,1,0:T(8,128)S(1)} reduce-window(s32[8,8,128]{2,1,0:T(8,128)S(1)} %fusion.22, s32[]{:T(128)} %constant.11.clone.1), window={size=1x1x128 pad=0_0x0_0x127_0}, to_apply=%region_0.0 | reduce-window | flops 1040384 | bytes 65540 | tf_op jit(solution)/shard_map/reduce-window
  4.9 0.3 slice_reduce_fusion
  5.2 0.2 reduce-window.9
  5.3 0.1 add_bitcast_fusion
  5.4 1.0 %bitcast_convert_fusion = f32[128,1024]{1,0:T(8,128)S(1)} fusion(bf16[1,1,128,1024]{3,2,1,0:T(8,128)(2,1)} %param.6), kind=kLoop, calls=%fused_computation.26 | loop fusion | flops 131072 | bytes 786432 | tf_op jit(solution)/shard_map/convert_element_type | solution.py:36
  6.4 0.8 copy.12
  7.2 0.1 mul.50
  7.3 7.2 %scatter_custom_fusion = bf16[1024,1024]{1,0:T(8,128)(2,1)} fusion(s32[1024]{0:T(1024)S(1)} %bitcast.68, f32[128,1024]{1,0:T(8,128)S(1)} %bitcast_convert_fusion, f32[1024]{0:T(1024)S(1)} %mul.50, bf16[]{:T(256)} %constant.9.clone.1), kind=kCustom, calls=%fused_computation.3 | custom fusion | flops 2097152 | bytes 2625538 | tf_op jit(solution)/shard_map/scatter | solution.py:47
  14.6 0.0 copy-start.2
  14.6 6.5 %all-to-all-start = ((bf16[8,128,1024]{2,1,0:T(8,128)(2,1)}), bf16[8,128,1024]{2,1,0:T(8,128)(2,1)S(1)}, u32[]{:S(2)}, u32[]{:S(2)}) async-start(bf16[8,128,1024]{2,1,0:T(8,128)(2,1)} %bitcast.5), calls=%async_computation | async-start | bytes 4194304 | tf_op jit(solution)/shard_map/all_to_all | solution.py:49
  21.0 0.0 copy-done.2
  21.1 0.3 broadcast_in_dim.19
  21.4 2.1 %fusion.6 = bf16[256,1024]{1,0:T(8,128)(2,1)} fusion(f32[32,8,8,128]{3,2,1,0:T(8,128)S(1)} %bitcast.62, bf16[1,1,256,1024]{3,2,1,0:T(8,128)(2,1)} %param.10), kind=kLoop, calls=%fused_computation.9 | loop fusion | flops 786432 | bytes 2097152 | tf_op jit(solution)/shard_map/convert_element_type | solution.py:32
  23.5 1.5 %collective-permute-start = (bf16[256,1024]{1,0:T(8,128)(2,1)}, bf16[256,1024]{1,0:T(8,128)(2,1)}, u32[]{:S(2)}, u32[]{:S(2)}) collective-permute-start(bf16[256,1024]{1,0:T(8,128)(2,1)} %fusion.6), channel_id=1, source_target_pairs={{0,16},{16,0},{8,24},{24,8},{1,17},{17,1},{9,25},{25,9},{2,18},{18... | collective-permute-start | bytes 1572872 | tf_op jit(solution)/shard_map/ppermute | solution.py:17
  25.0 45.1 %all-to-all-done = bf16[8,128,1024]{2,1,0:T(8,128)(2,1)S(1)} async-done(((bf16[8,128,1024]{2,1,0:T(8,128)(2,1)}), bf16[8,128,1024]{2,1,0:T(8,128)(2,1)S(1)}, u32[]{:S(2)}, u32[]{:S(2)}) %all-to-all-start) | async-done | bytes 2097184 | tf_op jit(solution)/shard_map/all_to_all | solution.py:49
  70.1 0.0 copy-done
  70.1 1.3 %fusion.12 = bf16[1024,512]{1,0:T(8,128)(2,1)S(1)} fusion(bf16[1024,1024]{1,0:T(8,128)(2,1)S(1)} %bitcast.63, bf16[1,1,1,1024,512]{4,3,2,1,0:T(8,128)(2,1)S(1)} %copy-done), kind=kOutput, calls=%fused_computation.16 | convolution fusion | flops 1073741824 | bytes 4194304 | tf_op jit(solution)/shard_map/dot_general | solution.py:71
  71.4 1.1 %fusion.16 = (bf16[256,1024]{0,1:T(8,128)(2,1)}, bf16[256,1024]{0,1:T(8,128)(2,1)}) fusion(bf16[1024,512]{1,0:T(8,128)(2,1)S(1)} %fusion.12, s32[]{:T(128)S(6)} %mul.56, s32[]{:T(128)S(6)} %select_n.25), kind=kLoop, calls=%fused_computation.23 | loop fusion | bytes 2097160 | tf_op jit(solution)/shard_map/convert_element_type | solution.py:79
  72.5 1.5 %collective-permute-start.1 = (bf16[256,1024]{0,1:T(8,128)(2,1)}, bf16[256,1024]{0,1:T(8,128)(2,1)}, u32[]{:S(2)}, u32[]{:S(2)}) collective-permute-start(bf16[256,1024]{0,1:T(8,128)(2,1)} %get-tuple-element.7), channel_id=1, source_target_pairs={{0,16},{16,0},{8,24},{24,8},{1,17},{17,1},{9,25},{25,9},{2,18},{18... | collective-permute-start | bytes 1572872 | tf_op jit(solution)/shard_map/ppermute | solution.py:17
  74.0 0.0 collective-permute-done
  74.0 3.8 %fusion.5 = bf16[1,1,1,1024,512]{4,3,2,1,0:T(8,128)(2,1)} fusion(bf16[1024,1024]{1,0:T(8,128)(2,1)S(1)} %bitcast.64, bf16[256,1024]{1,0:T(8,128)(2,1)} %fusion.6, bf16[256,1024]{1,0:T(8,128)(2,1)} %collective-permute-done, pred[]{:T(512)S(6)} %eq.36), kind=kOutput, calls=%fused_computation.7 | convolution fusion | flops 1078984704 | bytes 4194305 | tf_op jit(solution)/shard_map/dot_general | solution.py:68
  77.8 8.4 %collective-permute-done.1 = bf16[256,1024]{0,1:T(8,128)(2,1)} collective-permute-done((bf16[256,1024]{0,1:T(8,128)(2,1)}, bf16[256,1024]{0,1:T(8,128)(2,1)}, u32[]{:S(2)}, u32[]{:S(2)}) %collective-permute-start.1) | collective-permute-done | bytes 524320 | tf_op jit(solution)/shard_map/ppermute | solution.py:17
  86.2 0.0 copy-done.1
  86.2 1.2 %fusion.18 = bf16[1,1,256,1024]{2,3,1,0:T(8,128)(2,1)S(1)} fusion(bf16[256,1024]{0,1:T(8,128)(2,1)} %collective-permute-done.1, bf16[256,1024]{0,1:T(8,128)(2,1)S(1)} %copy-done.1), kind=kLoop, calls=%fused_computation.25 | loop fusion | flops 1048576 | bytes 1572864 | tf_op jit(solution)/shard_map/broadcast_in_dim | solution.py:82
  87.4 1.0 %copy.13 = bf16[1,1,256,1024]{3,2,1,0:T(8,128)(2,1)} copy(bf16[1,1,256,1024]{2,3,1,0:T(8,128)(2,1)S(1)} %fusion.18) | data formatting | bytes 1048576
  (5 shorter events, 0.0 us)
Async XLA Ops:
  0.6 69.5 %copy-start = (bf16[1,1,1,1024,512]{4,3,2,1,0:T(8,128)(2,1)S(1)}, bf16[1,1,1,1024,512]{4,3,2,1,0:T(8,128)(2,1)}, u32[]{:S(2)}) copy-start(bf16[1,1,1,1024,512]{4,3,2,1,0:T(8,128)(2,1)} %param.9) | copy-start | bytes 3145732
  14.6 6.5 %copy-start.2 = (f32[1,1,2,8]{3,2,1,0:T(2,128)S(1)}, f32[1,1,2,8]{3,2,1,0:T(2,128)}, u32[]{:S(2)}) copy-start(f32[1,1,2,8]{3,2,1,0:T(2,128)} %param.11) | copy-start | bytes 196
  14.6 55.5 %all-to-all-start = ((bf16[8,128,1024]{2,1,0:T(8,128)(2,1)}), bf16[8,128,1024]{2,1,0:T(8,128)(2,1)S(1)}, u32[]{:S(2)}, u32[]{:S(2)}) async-start(bf16[8,128,1024]{2,1,0:T(8,128)(2,1)} %bitcast.5), calls=%async_computation | async-start | bytes 4194304 | tf_op jit(solution)/shard_map/all_to_all | solution.py:49
  23.5 50.5 %collective-permute-start = (bf16[256,1024]{1,0:T(8,128)(2,1)}, bf16[256,1024]{1,0:T(8,128)(2,1)}, u32[]{:S(2)}, u32[]{:S(2)}) collective-permute-start(bf16[256,1024]{1,0:T(8,128)(2,1)} %fusion.6), channel_id=1, source_target_pairs={{0,16},{16,0},{8,24},{24,8},{1,17},{17,1},{9,25},{25,9},{2,18},{18... | collective-permute-start | bytes 1572872 | tf_op jit(solution)/shard_map/ppermute | solution.py:17
  72.5 13.8 %collective-permute-start.1 = (bf16[256,1024]{0,1:T(8,128)(2,1)}, bf16[256,1024]{0,1:T(8,128)(2,1)}, u32[]{:S(2)}, u32[]{:S(2)}) collective-permute-start(bf16[256,1024]{0,1:T(8,128)(2,1)} %get-tuple-element.7), channel_id=1, source_target_pairs={{0,16},{16,0},{8,24},{24,8},{1,17},{17,1},{9,25},{25,9},{2,18},{18... | collective-permute-start | bytes 1572872 | tf_op jit(solution)/shard_map/ppermute | solution.py:17
  74.0 12.3 %copy-start.1 = (bf16[256,1024]{0,1:T(8,128)(2,1)S(1)}, bf16[256,1024]{0,1:T(8,128)(2,1)}, u32[]{:S(2)}) copy-start(bf16[256,1024]{0,1:T(8,128)(2,1)} %get-tuple-element.6) | copy-start | bytes 1572868
where the time goes:
time: 88.9 us; the launch traced here: 88.4 us
  waiting for transfers between devices  53.5 us (60%)
  other arithmetic  14.9 us (17%)
  starting transfers between devices  9.49 us (11%)
  matrix products  5.12 us (6%)
  local copies, waits for them, and re-layouts  4.76 us (5%)
    all_to_all x1, waiting for transfers between devices, on_device(): lax.all_to_all(filled.reshape(experts, capacity, D), 'expert', split_axis...  45.1 us
    ppermute x2, waiting for transfers between devices, partner(): return lax.ppermute(block, axis, route)  8.43 us
    scatter x1, other arithmetic, on_device(): jnp.zeros((experts * capacity, D), jnp.bfloat16).at[slot_index].set(scaled)  7.24 us
    all_to_all x1, starting transfers between devices, on_device(): lax.all_to_all(filled.reshape(experts, capacity, D), 'expert', split_axis...  6.46 us
    dot_general x1, matrix products, on_device(): lax.dot_general(rows_stack, whole, row_dims, preferred_element_type=jnp.f...  3.84 us
    ppermute x2, starting transfers between devices, partner(): return lax.ppermute(block, axis, route)  3.03 us
    unnamed x9, local copies, waits for them, and re-layouts  2.6 us
    another operation x2, other arithmetic  2.43 us
  transfers between devices with their start and end apart: 3, of which 2 were waited for; matrix products, arithmetic and copies ran while one was open for 10% of the time, Pallas kernels for 0%

commit v1 on v0

v1 whole, which is shorter than its diff:
```python
import functools

import jax
import jax.numpy as jnp
from jax import lax
from jax.experimental import pallas as pl
from jax.experimental.pallas import tpu as pltpu
from jax.sharding import PartitionSpec as P

QBLOCK = 128
WIDTH = 256
MESH = pl.DeviceIdType.MESH


def partner(block, axis):
    count = lax.axis_size(axis)
    route = [(place, (place + count // 2) % count) for place in range(count)]
    return lax.ppermute(block, axis, route)


def expand(scales):
    return jnp.repeat(jnp.repeat(scales, QBLOCK, axis=0), QBLOCK, axis=1)


def general(gradient, gate_rows, route_rows, activations, weight, scales):
    experts = lax.axis_size("expert")
    tok_count, features = gradient.shape
    top_count = route_rows.shape[1]
    capacity = tok_count * top_count // experts
    dequant_half = (weight.astype(jnp.float32) * expand(scales)).astype(jnp.bfloat16)
    named = route_rows[:, :, None] == jnp.arange(experts, dtype=jnp.int32)[None, None, :]
    gate_of = jnp.sum(jnp.where(named, gate_rows[:, :, None], 0.0), axis=1)
    member = jnp.any(named, axis=1)
    earlier = jnp.tril(jnp.ones((tok_count, tok_count), jnp.bfloat16), -1)
    rank = jnp.dot(earlier, member.astype(jnp.bfloat16), preferred_element_type=jnp.float32)
    rank = rank.astype(jnp.int32)
    places = jnp.arange(capacity, dtype=jnp.int32)[None, :, None]
    picked = member.T[:, None, :] & (rank.T[:, None, :] == places)
    slot_gate = jnp.sum(jnp.where(picked, gate_of.T[:, None, :], 0.0), axis=2)
    rows = jnp.dot(
        picked.reshape(experts * capacity, tok_count).astype(jnp.bfloat16),
        gradient,
        preferred_element_type=jnp.float32,
    )
    filled = (slot_gate.reshape(experts * capacity, 1) * rows).astype(jnp.bfloat16)
    received = lax.all_to_all(
        filled.reshape(experts, capacity, features),
        "expert",
        split_axis=0,
        concat_axis=0,
        tiled=True,
    ).reshape(experts * capacity, features)
    half_size = lax.axis_size("pipe") // 2
    upper_half = (lax.axis_index("pipe") >= half_size).astype(jnp.int32)
    half_rows = dequant_half.shape[0]
    other_half = partner(dequant_half, "pipe")
    whole = jnp.where(
        upper_half == 1,
        jnp.concatenate([other_half, dequant_half], axis=0),
        jnp.concatenate([dequant_half, other_half], axis=0),
    )
    hidden = lax.dot_general(
        received, whole, (((1,), (1,)), ((), ())), preferred_element_type=jnp.float32
    ).astype(jnp.bfloat16)
    section_sum = lax.dot_general(
        activations, received, (((0,), (0,)), ((), ())), preferred_element_type=jnp.float32
    )
    their_part = lax.dynamic_slice_in_dim(
        section_sum, (1 - upper_half) * half_rows, half_rows, 0
    ).astype(jnp.bfloat16)
    received_part = partner(their_part, "pipe")
    own_part = lax.dynamic_slice_in_dim(section_sum, upper_half * half_rows, half_rows, 0)
    rounded = lax.optimization_barrier(own_part.astype(jnp.bfloat16)).astype(jnp.float32)
    weight_grad = (rounded + received_part.astype(jnp.float32)).astype(jnp.bfloat16)
    return hidden, weight_grad


def kernel(
    sections, experts, gates_ref, routes_ref, scales_ref, x_hbm, act_hbm, weight_hbm,
    hidden_hbm, grad_hbm,
    x_own, act, act_t, weight, whole, got, scaled, gate_out, gate_in, gate_wide,
    theirs, ours, arrived, hidden, grad,
    load_sem, store_sem, row_send, row_recv, gate_send, gate_recv, w_send, w_recv, p_send, p_recv,
):
    section = lax.axis_index("pipe")
    me = lax.axis_index("expert")
    pair = lax.rem(section + sections // 2, sections)
    upper = section // (sections // 2)
    high, core = me // 2, lax.rem(me, 2)
    sibling = me + 1 - 2 * core
    last = experts // 2 - 1
    tokens, features = x_hbm.shape
    chunks = features // WIDTH
    slots, wide = act_hbm.shape
    half = wide // 2

    def rows_of(block):
        return pl.ds(pl.multiple_of(block * tokens, tokens), tokens)

    def columns(chunk):
        return pl.ds(pl.multiple_of(chunk * WIDTH, WIDTH), WIDTH)

    load_x = pltpu.make_async_copy(x_hbm, x_own, load_sem.at[0])
    load_w = pltpu.make_async_copy(weight_hbm, weight, load_sem.at[1])
    load_a = pltpu.make_async_copy(act_hbm, act, load_sem.at[2])
    load_x.start()
    load_w.start()
    load_a.start()

    barrier = pltpu.get_barrier_semaphore()
    for step in range(1, experts):
        peer = lax.rem(me + step, experts)
        pl.semaphore_signal(barrier, inc=1, device_id=(section, peer), device_id_type=MESH)
    pl.semaphore_signal(barrier, inc=1, device_id=(pair, me), device_id_type=MESH)

    for expert in range(experts):
        gate_out[expert] = jnp.sum(
            jnp.where(routes_ref[...] == expert, gates_ref[...], 0.0), axis=0, keepdims=True
        )
    gate_in[me] = gate_out[me]
    load_x.wait()
    pl.semaphore_wait(barrier, experts)

    def move(block, chunk, way, peer, from_own=False):
        source = x_own.at[:, columns(chunk)] if from_own else got.at[chunk, rows_of(block)]
        return pltpu.make_async_remote_copy(
            src_ref=source,
            dst_ref=got.at[chunk, rows_of(block)],
            send_sem=row_send.at[way, block, chunk],
            recv_sem=row_recv.at[block, chunk],
            device_id=(section, peer),
            device_id_type=MESH,
        )

    def send_own(chunk):
        @pl.when(high > 0)
        def _():
            move(me, chunk, 0, me - 2, True).start()

        @pl.when(high < last)
        def _():
            move(me, chunk, 1, me + 2, True).start()

        move(me, chunk, 2, sibling, True).start()

    def gate_copy(peer, source):
        return pltpu.make_async_remote_copy(
            src_ref=gate_out.at[peer],
            dst_ref=gate_in.at[source],
            send_sem=gate_send.at[peer],
            recv_sem=gate_recv.at[source],
            device_id=(section, peer),
            device_id_type=MESH,
        )

    def weight_copy(chunk, which):
        rows = pl.ds(pl.multiple_of(which * half, half), half)
        return pltpu.make_async_remote_copy(
            src_ref=whole.at[chunk, rows],
            dst_ref=whole.at[chunk, rows],
            send_sem=w_send.at[chunk],
            recv_sem=w_recv.at[chunk],
            device_id=(pair, me),
            device_id_type=MESH,
        )

    def part_copy(chunk):
        return pltpu.make_async_remote_copy(
            src_ref=theirs.at[chunk],
            dst_ref=arrived.at[chunk],
            send_sem=p_send.at[chunk],
            recv_sem=p_recv.at[chunk],
            device_id=(pair, me),
            device_id_type=MESH,
        )

    for step in range(1, experts):
        gate_copy(lax.rem(me + step, experts), me).start()
    send_own(0)
    send_own(1)

    load_w.wait()
    for chunk in range(chunks):
        for row in range(half // QBLOCK):
            for part in range(WIDTH // QBLOCK):
                column = chunk * (WIDTH // QBLOCK) + part
                piece = weight[
                    row * QBLOCK : (row + 1) * QBLOCK, column * QBLOCK : (column + 1) * QBLOCK
                ]
                whole[
                    chunk,
                    pl.ds(pl.multiple_of(upper * half + row * QBLOCK, QBLOCK), QBLOCK),
                    part * QBLOCK : (part + 1) * QBLOCK,
                ] = (piece.astype(jnp.float32) * scales_ref[row, column]).astype(jnp.bfloat16)
        weight_copy(chunk, upper).start()

    load_a.wait()

    @pl.loop(0, slots // WIDTH)
    def _(tile):
        at = pl.ds(pl.multiple_of(tile * WIDTH, WIDTH), WIDTH)
        act_t[:, at] = act[at, :].T

    for step in range(1, experts):
        source = lax.rem(me + step, experts)
        gate_copy(source, source).wait_recv()

    for block in range(experts):
        gate_wide[block] = jnp.broadcast_to(gate_in[block], (QBLOCK, tokens)).T

    def apply_gate(block, chunk, rows):
        for part in range(WIDTH // QBLOCK):
            at = slice(part * QBLOCK, (part + 1) * QBLOCK)
            scaled[chunk, rows_of(block), at] = (
                gate_wide[block] * rows[:, at].astype(jnp.float32)
            ).astype(jnp.bfloat16)

    def landed(block, chunk):
        move(block, chunk, 2, sibling).wait_recv()

    def gate_landed(block, chunk):
        apply_gate(block, chunk, got[chunk, rows_of(block)])

    @pl.loop(0, chunks)
    def _(chunk):
        apply_gate(me, chunk, x_own[:, columns(chunk)])
        for step in range(1, experts // 2):
            @pl.when(high >= step)
            def _():
                block = me - 2 * step
                landed(block, chunk)

                @pl.when(high < last)
                def _():
                    move(block, chunk, 1, me + 2).start()

                move(block, chunk, 2, sibling).start()

            @pl.when(high + step <= last)
            def _():
                block = me + 2 * step
                landed(block, chunk)

                @pl.when(high > 0)
                def _():
                    move(block, chunk, 0, me - 2).start()

                move(block, chunk, 2, sibling).start()

            if step == 1:
                landed(sibling, chunk)
                gate_landed(sibling, chunk)

            @pl.when(high >= step)
            def _():
                block = me - 2 * step
                gate_landed(block, chunk)

            @pl.when(high + step <= last)
            def _():
                block = me + 2 * step
                gate_landed(block, chunk)

        @pl.when(chunk + 2 < chunks)
        def _():
            send_own(chunk + 2)

        for step in range(1, experts // 2):
            @pl.when(high >= step)
            def _():
                block = sibling - 2 * step
                landed(block, chunk)
                gate_landed(block, chunk)

            @pl.when(high + step <= last)
            def _():
                block = sibling + 2 * step
                landed(block, chunk)
                gate_landed(block, chunk)

        their_rows = pl.ds(pl.multiple_of((1 - upper) * half, half), half)
        theirs[chunk] = jnp.dot(
            act_t[their_rows, :], scaled[chunk], preferred_element_type=jnp.float32
        ).astype(jnp.bfloat16)
        part_copy(chunk).start()
        our_rows = pl.ds(pl.multiple_of(upper * half, half), half)
        ours[chunk] = jnp.dot(
            act_t[our_rows, :], scaled[chunk], preferred_element_type=jnp.float32
        ).astype(jnp.bfloat16)

    for chunk in range(chunks):
        weight_copy(chunk, 1 - upper).wait_recv()

    @pl.loop(0, slots // WIDTH)
    def _(tile):
        at = pl.ds(pl.multiple_of(tile * WIDTH, WIDTH), WIDTH)
        total = None
        for chunk in range(chunks):
            term = lax.dot_general(
                scaled[chunk, at],
                whole[chunk],
                (((1,), (1,)), ((), ())),
                preferred_element_type=jnp.float32,
            )
            total = term if total is None else total + term
        hidden[at, :] = total.astype(jnp.bfloat16)

    store_h = pltpu.make_async_copy(hidden, hidden_hbm, store_sem.at[0])
    store_h.start()

    for chunk in range(chunks):
        part_copy(chunk).wait_recv()
        grad[:, chunk * WIDTH : (chunk + 1) * WIDTH] = (
            ours[chunk].astype(jnp.float32) + arrived[chunk].astype(jnp.float32)
        ).astype(jnp.bfloat16)
    store_g = pltpu.make_async_copy(grad, grad_hbm, store_sem.at[1])
    store_g.start()

    for step in range(1, experts):
        gate_copy(lax.rem(me + step, experts), me).wait_send()

    @pl.loop(0, chunks)
    def _(chunk):
        part_copy(chunk).wait_send()
        weight_copy(chunk, upper).wait_send()

        @pl.when(high > 0)
        def _():
            move(me, chunk, 0, me - 2, True).wait_send()

        @pl.when(high < last)
        def _():
            move(me, chunk, 1, me + 2, True).wait_send()

        move(me, chunk, 2, sibling, True).wait_send()
        for step in range(1, experts // 2):
            @pl.when(high >= step)
            def _():
                block = me - 2 * step

                @pl.when(high < last)
                def _():
                    move(block, chunk, 1, me + 2).wait_send()

                move(block, chunk, 2, sibling).wait_send()

            @pl.when(high + step <= last)
            def _():
                block = me + 2 * step

                @pl.when(high > 0)
                def _():
                    move(block, chunk, 0, me - 2).wait_send()

                move(block, chunk, 2, sibling).wait_send()

    store_h.wait()
    store_g.wait()


def every_expert(gradient, gate_rows, route_rows, activations, weight, scales):
    sections, experts = lax.axis_size("pipe"), lax.axis_size("expert")
    tokens, features = gradient.shape
    slots, wide = activations.shape
    half = weight.shape[0]
    chunks = features // WIDTH
    bf16, f32 = jnp.bfloat16, jnp.float32
    dma = pltpu.SemaphoreType.DMA
    anywhere = pl.BlockSpec(memory_space=pl.ANY)
    vmem = pl.BlockSpec(memory_space=pltpu.VMEM)
    return pl.pallas_call(
        functools.partial(kernel, sections, experts),
        out_shape=(
            jax.ShapeDtypeStruct((slots, wide), bf16),
            jax.ShapeDtypeStruct((half, features), bf16),
        ),
        in_specs=[
            vmem, vmem, pl.BlockSpec(memory_space=pltpu.SMEM), anywhere, anywhere, anywhere,
        ],
        out_specs=(anywhere, anywhere),
        scratch_shapes=[
            pltpu.VMEM((tokens, features), bf16),
            pltpu.VMEM((slots, wide), bf16),
            pltpu.VMEM((wide, slots), bf16),
            pltpu.VMEM((half, features), bf16),
            pltpu.VMEM((chunks, wide, WIDTH), bf16),
            pltpu.VMEM((chunks, slots, WIDTH), bf16),
            pltpu.VMEM((chunks, slots, WIDTH), bf16),
            pltpu.VMEM((experts, 1, tokens), f32),
            pltpu.VMEM((experts, 1, tokens), f32),
            pltpu.VMEM((experts, tokens, QBLOCK), f32),
            pltpu.VMEM((chunks, half, WIDTH), bf16),
            pltpu.VMEM((chunks, half, WIDTH), bf16),
            pltpu.VMEM((chunks, half, WIDTH), bf16),
            pltpu.VMEM((slots, wide), bf16),
            pltpu.VMEM((half, features), bf16),
            dma((3,)),
            dma((2,)),
            dma((3, experts, chunks)),
            dma((experts, chunks)),
            dma((experts,)),
            dma((experts,)),
            dma((chunks,)),
            dma((chunks,)),
            dma((chunks,)),
            dma((chunks,)),
        ],
        compiler_params=pltpu.CompilerParams(
            collective_id=0, has_side_effects=True, vmem_limit_bytes=48 * 2**20
        ),
        cost_estimate=pl.CostEstimate(
            flops=4 * slots * wide * features,
            bytes_accessed=4 * slots * wide + 6 * half * features,
            transcendentals=0,
        ),
    )(gate_rows.T, route_rows.T, scales, gradient, activations, weight)


def on_device(out_grad, gate_weights, routes, hidden_act, down_weight, block_scales):
    experts, sections = lax.axis_size("expert"), lax.axis_size("pipe")
    gradient, gate_rows, route_rows = out_grad[0, 0], gate_weights[0, 0], routes[0, 0]
    weight, scales = down_weight[0, 0], block_scales[0, 0]
    tokens, features = gradient.shape
    dense = (
        experts == route_rows.shape[1]
        and experts >= 4
        and experts % 2 == 0
        and sections % 2 == 0
        and tokens == QBLOCK
        and features % WIDTH == 0
        and features // WIDTH >= 2
        and weight.shape[0] % QBLOCK == 0
    )
    form = every_expert if dense else general
    hidden, weight_grad = form(
        gradient, gate_rows, route_rows, hidden_act[0, 0, 0], weight, scales
    )
    return hidden[None, None, None], weight_grad[None, None]


def solution(mesh):
    in_specs = (
        P("pipe", None, "expert", None),
        P("pipe", None, "expert", None),
        P("pipe", None, "expert", None),
        P("pipe", None, "expert", None, None),
        P("pipe", "expert", None, None),
        P("pipe", "expert", None, None),
    )
    out_specs = (P("pipe", None, "expert", None, None), P("pipe", "expert", None, None))
    return jax.shard_map(
        on_device, mesh=mesh, in_specs=in_specs, out_specs=out_specs, check_vma=False
    )
```

time: 88.9 us -> 46.5 us (0.52)
  waiting for transfers between devices: 53.5 us -> 0 us
  Pallas kernels: 0 us -> 39.9 us
  other arithmetic: 14.9 us -> 0 us
  starting transfers between devices: 9.49 us -> 0 us
  matrix products: 5.12 us -> 0 us
  local copies, waits for them, and re-layouts: 4.76 us -> 5.67 us
    all_to_all x1 -> x0, waiting for transfers between devices: 45.1 us -> none  [on_device(): lax.all_to_all(filled.reshape(experts, capacity, D), 'expert', split_axis...]
    pallas_call x0 -> x1, Pallas kernels: none -> 39.9 us  [every_expert(): pl.pallas_call(functools.partial(kernel, sections, experts), out_shape=(j...]
    ppermute x2 -> x0, waiting for transfers between devices: 8.43 us -> none  [partner(): return lax.ppermute(block, axis, route)]
    scatter x1 -> x0, other arithmetic: 7.24 us -> none  [on_device(): jnp.zeros((experts * capacity, D), jnp.bfloat16).at[slot_index].set(scaled)]
    all_to_all x1 -> x0, starting transfers between devices: 6.46 us -> none  [on_device(): lax.all_to_all(filled.reshape(experts, capacity, D), 'expert', split_axis...]
    dot_general x2 -> x0, matrix products: 5.12 us -> none  [the longest x1 3.84 us: on_device(): lax.dot_general(rows_stack, whole, row_dims, preferred_element_type=jnp.f...]
    convert_element_type x3 -> x0, other arithmetic: 3.13 us -> none  [the longest x1 2.13 us: on_device(): (down_weight[0, 0].astype(jnp.float32) * expand(block_scales[0, 0])).asty...]
    unnamed x9 -> x14, local copies, waits for them, and re-layouts: 2.6 us -> 5.67 us
  transfers between devices with their start and end apart: 3 -> 0, of which waited for: 2 -> 0; matrix products, arithmetic and copies ran while one was open for 10% -> 0% of each run, Pallas kernels for 0% -> 0%
where the time goes in v1:
time: 46.5 us; the launch traced here: 46.2 us
  Pallas kernels  39.9 us (86%)
  local copies, waits for them, and re-layouts  5.67 us (12%)
  between operations  0.67 us (1%)
    pallas_call x1, Pallas kernels, every_expert(): pl.pallas_call(functools.partial(kernel, sections, experts), out_shape=(j...  39.9 us
    unnamed x14, local copies, waits for them, and re-layouts  5.67 us

profile of v1, /device:TPU:0, one launch (start us, length us, event | category | flops | bytes accessed | tf_op | source)
XLA Modules:
  0.0 46.2 jit_solution(4998144633023721877)
XLA Ops:
  0.6 0.0 copy-start.4
  0.6 0.0 copy-start.3
  0.7 0.0 copy-start.5
  0.7 0.7 %copy-done.4 = s32[1,1,128,8]{2,3,1,0:T(8,128)S(1)} copy-done((s32[1,1,128,8]{2,3,1,0:T(8,128)S(1)}, s32[1,1,128,8]{2,3,1,0:T(8,128)}, u32[]{:S(2)}) %copy-start.4) | copy-done | bytes 4120
  1.3 0.0 copy-done.3
  1.3 0.0 copy-done.5
  1.3 0.0 copy-start
  1.3 1.2 %copy-done = bf16[1,1,1,1024,512]{4,3,2,1,0:T(8,128)(2,1)S(1)} copy-done((bf16[1,1,1,1024,512]{4,3,2,1,0:T(8,128)(2,1)S(1)}, bf16[1,1,1,1024,512]{4,3,2,1,0:T(8,128)(2,1)}, u32[]{:S(2)}) %copy-start) | copy-done | bytes 1048600
  2.6 0.0 copy-start.1
  2.6 1.0 %copy-done.1 = bf16[1,1,256,1024]{3,2,1,0:T(8,128)(2,1)S(1)} copy-done((bf16[1,1,256,1024]{3,2,1,0:T(8,128)(2,1)S(1)}, bf16[1,1,256,1024]{3,2,1,0:T(8,128)(2,1)}, u32[]{:S(2)}) %copy-start.1) | copy-done | bytes 524312
  3.6 0.0 copy-start.2
  3.6 0.9 %copy-done.2 = bf16[1,1,128,1024]{3,2,1,0:T(8,128)(2,1)S(1)} copy-done((bf16[1,1,128,1024]{3,2,1,0:T(8,128)(2,1)S(1)}, bf16[1,1,128,1024]{3,2,1,0:T(8,128)(2,1)}, u32[]{:S(2)}) %copy-start.2) | copy-done | bytes 262168
  4.6 39.9 %shard_map.77 = (bf16[1024,512]{1,0:T(8,128)(2,1)S(1)}, bf16[256,1024]{1,0:T(8,128)(2,1)S(1)}) custom-call(f32[8,128]{1,0:T(8,128)S(1)} %bitcast.17, s32[8,128]{1,0:T(8,128)S(1)} %bitcast.18, f32[2,8]{1,0:T(2,128)S(1)} %bitcast.19, bf16[128,1024]{1,0:T(8,128)(2,1)S(1)} %bitcast.16, bf16[1024,512]{1,0:T(8,128)(2,1)S(1)} %bitcast.14, ...), custom_call_target="tpu_custom_call" | custom-call | flops 2147483648 | bytes 3670016 | tf_op jit(solution)/shard_map/pallas_call | solution.py:371
  44.5 1.0 %copy.10 = bf16[1,1,1,1024,512]{4,3,2,1,0:T(8,128)(2,1)} copy(bf16[1,1,1,1024,512]{4,3,2,1,0:T(8,128)(2,1)S(1)} %bitcast.12) | data formatting | bytes 2097152
  45.4 0.8 %copy.11 = bf16[1,1,256,1024]{3,2,1,0:T(8,128)(2,1)} copy(bf16[1,1,256,1024]{3,2,1,0:T(8,128)(2,1)S(1)} %bitcast.13) | data formatting | bytes 1048576
Async XLA Ops:
  0.6 0.7 %copy-start.4 = (s32[1,1,128,8]{2,3,1,0:T(8,128)S(1)}, s32[1,1,128,8]{2,3,1,0:T(8,128)}, u32[]{:S(2)}) copy-start(s32[1,1,128,8]{2,3,1,0:T(8,128)} %param.8) | copy-start | bytes 12292
  0.6 0.7 %copy-start.3 = (f32[1,1,128,8]{2,3,1,0:T(8,128)S(1)}, f32[1,1,128,8]{2,3,1,0:T(8,128)}, u32[]{:S(2)}) copy-start(f32[1,1,128,8]{2,3,1,0:T(8,128)} %param.7) | copy-start | bytes 12292
  0.7 0.7 %copy-start.5 = (f32[1,1,2,8]{3,2,1,0:T(2,128)S(1)}, f32[1,1,2,8]{3,2,1,0:T(2,128)}, u32[]{:S(2)}) copy-start(f32[1,1,2,8]{3,2,1,0:T(2,128)} %param.11) | copy-start | bytes 196
  1.3 1.2 %copy-start = (bf16[1,1,1,1024,512]{4,3,2,1,0:T(8,128)(2,1)S(1)}, bf16[1,1,1,1024,512]{4,3,2,1,0:T(8,128)(2,1)}, u32[]{:S(2)}) copy-start(bf16[1,1,1,1024,512]{4,3,2,1,0:T(8,128)(2,1)} %param.9) | copy-start | bytes 3145732
  2.6 1.0 %copy-start.1 = (bf16[1,1,256,1024]{3,2,1,0:T(8,128)(2,1)S(1)}, bf16[1,1,256,1024]{3,2,1,0:T(8,128)(2,1)}, u32[]{:S(2)}) copy-start(bf16[1,1,256,1024]{3,2,1,0:T(8,128)(2,1)} %param.10) | copy-start | bytes 1572868
  3.6 0.9 %copy-start.2 = (bf16[1,1,128,1024]{3,2,1,0:T(8,128)(2,1)S(1)}, bf16[1,1,128,1024]{3,2,1,0:T(8,128)(2,1)}, u32[]{:S(2)}) copy-start(bf16[1,1,128,1024]{3,2,1,0:T(8,128)(2,1)} %param.6) | copy-start | bytes 786436

commit v2 on v1

--- a/solution.py
+++ b/solution.py
@@ -9,6 +9,7 @@
 
 QBLOCK = 128
 WIDTH = 256
+ROOM = 63 * 2**20
 MESH = pl.DeviceIdType.MESH
 
 
@@ -76,10 +77,10 @@
 
 
 def kernel(
-    sections, experts, gates_ref, routes_ref, scales_ref, x_hbm, act_hbm, weight_hbm,
+    sections, experts, gates_hbm, routes_hbm, scales_hbm, x_hbm, act_hbm, weight_hbm,
     hidden_hbm, grad_hbm,
-    x_own, act, act_t, weight, whole, got, scaled, gate_out, gate_in, gate_wide,
-    theirs, ours, arrived, hidden, grad,
+    gates_ref, routes_ref, scales_ref, hidden_ref, grad_ref, x_own, act, act_t, weight, whole, got, scaled, gate_out, gate_in, gate_wide,
+    theirs, ours, arrived,
     load_sem, store_sem, row_send, row_recv, gate_send, gate_recv, w_send, w_recv, p_send, p_recv,
 ):
     section = lax.axis_index("pipe")
@@ -103,9 +104,11 @@
     load_x = pltpu.make_async_copy(x_hbm, x_own, load_sem.at[0])
     load_w = pltpu.make_async_copy(weight_hbm, weight, load_sem.at[1])
     load_a = pltpu.make_async_copy(act_hbm, act, load_sem.at[2])
-    load_x.start()
-    load_w.start()
-    load_a.start()
+    load_g = pltpu.make_async_copy(gates_hbm, gates_ref, load_sem.at[3])
+    load_r = pltpu.make_async_copy(routes_hbm, routes_ref, load_sem.at[4])
+    load_s = pltpu.make_async_copy(scales_hbm, scales_ref, load_sem.at[5])
+    for load in (load_x, load_w, load_s, load_g, load_r, load_a):
+        load.start()
 
     barrier = pltpu.get_barrier_semaphore()
     for step in range(1, experts):
@@ -113,11 +116,6 @@
         pl.semaphore_signal(barrier, inc=1, device_id=(section, peer), device_id_type=MESH)
     pl.semaphore_signal(barrier, inc=1, device_id=(pair, me), device_id_type=MESH)
 
-    for expert in range(experts):
-        gate_out[expert] = jnp.sum(
-            jnp.where(routes_ref[...] == expert, gates_ref[...], 0.0), axis=0, keepdims=True
-        )
-    gate_in[me] = gate_out[me]
     load_x.wait()
     pl.semaphore_wait(barrier, experts)
 
@@ -174,12 +172,11 @@
             device_id_type=MESH,
         )
 
-    for step in range(1, experts):
-        gate_copy(lax.rem(me + step, experts), me).start()
     send_own(0)
     send_own(1)
 
     load_w.wait()
+    load_s.wait()
     for chunk in range(chunks):
         for row in range(half // QBLOCK):
             for part in range(WIDTH // QBLOCK):
@@ -194,6 +191,16 @@
                 ] = (piece.astype(jnp.float32) * scales_ref[row, column]).astype(jnp.bfloat16)
         weight_copy(chunk, upper).start()
 
+    load_g.wait()
+    load_r.wait()
+    for expert in range(experts):
+        gate_out[expert] = jnp.sum(
+            jnp.where(routes_ref[...] == expert, gates_ref[...], 0.0), axis=0, keepdims=True
+        )
+    gate_in[me] = gate_out[me]
+    for step in range(1, experts):
+        gate_copy(lax.rem(me + step, experts), me).start()
+
     load_a.wait()
 
     @pl.loop(0, slots // WIDTH)
@@ -303,17 +310,17 @@
                 preferred_element_type=jnp.float32,
             )
             total = term if total is None else total + term
-        hidden[at, :] = total.astype(jnp.bfloat16)
-
-    store_h = pltpu.make_async_copy(hidden, hidden_hbm, store_sem.at[0])
+        hidden_ref[at, :] = total.astype(jnp.bfloat16)
+
+    store_h = pltpu.make_async_copy(hidden_ref, hidden_hbm, store_sem.at[0])
     store_h.start()
 
     for chunk in range(chunks):
         part_copy(chunk).wait_recv()
-        grad[:, chunk * WIDTH : (chunk + 1) * WIDTH] = (
+        grad_ref[:, chunk * WIDTH : (chunk + 1) * WIDTH] = (
             ours[chunk].astype(jnp.float32) + arrived[chunk].astype(jnp.float32)
         ).astype(jnp.bfloat16)
-    store_g = pltpu.make_async_copy(grad, grad_hbm, store_sem.at[1])
+    store_g = pltpu.make_async_copy(grad_ref, grad_hbm, store_sem.at[1])
     store_g.start()
 
     for step in range(1, experts):
@@ -356,6 +363,17 @@
 
     store_h.wait()
     store_g.wait()
+
+
+def store(hidden_ref, grad_ref, hidden_hbm, grad_hbm, sem):
+    copies = [
+        pltpu.make_async_copy(hidden_ref, hidden_hbm, sem.at[0]),
+        pltpu.make_async_copy(grad_ref, grad_hbm, sem.at[1]),
+    ]
+    for copy in copies:
+        copy.start()
+    for copy in copies:
+        copy.wait()
 
 
 def every_expert(gradient, gate_rows, route_rows, activations, weight, scales):
@@ -366,19 +384,21 @@
     chunks = features // WIDTH
     bf16, f32 = jnp.bfloat16, jnp.float32
     dma = pltpu.SemaphoreType.DMA
-    anywhere = pl.BlockSpec(memory_space=pl.ANY)
-    vmem = pl.BlockSpec(memory_space=pltpu.VMEM)
-    return pl.pallas_call(
+    shapes = (
+        jax.ShapeDtypeStruct((slots, wide), bf16),
+        jax.ShapeDtypeStruct((half, features), bf16),
+    )
+    results = pl.pallas_call(
         functools.partial(kernel, sections, experts),
-        out_shape=(
-            jax.ShapeDtypeStruct((slots, wide), bf16),
-            jax.ShapeDtypeStruct((half, features), bf16),
-        ),
-        in_specs=[
-            vmem, vmem, pl.BlockSpec(memory_space=pltpu.SMEM), anywhere, anywhere, anywhere,
-        ],
-        out_specs=(anywhere, anywhere),
+        out_shape=shapes,
+        in_specs=[pl.BlockSpec(memory_space=pltpu.HBM)] * 6,
+        out_specs=(pl.BlockSpec(memory_space=pltpu.HBM),) * 2,
         scratch_shapes=[
+            pltpu.VMEM(gate_rows.shape[::-1], f32),
+            pltpu.VMEM(route_rows.shape[::-1], jnp.int32),
+            pltpu.SMEM(scales.shape, f32),
+            pltpu.VMEM((slots, wide), bf16),
+            pltpu.VMEM((half, features), bf16),
             pltpu.VMEM((tokens, features), bf16),
             pltpu.VMEM((slots, wide), bf16),
             pltpu.VMEM((wide, slots), bf16),
@@ -392,9 +412,7 @@
             pltpu.VMEM((chunks, half, WIDTH), bf16),
             pltpu.VMEM((chunks, half, WIDTH), bf16),
             pltpu.VMEM((chunks, half, WIDTH), bf16),
-            pltpu.VMEM((slots, wide), bf16),
-            pltpu.VMEM((half, features), bf16),
-            dma((3,)),
+            dma((6,)),
             dma((2,)),
             dma((3, experts, chunks)),
             dma((experts, chunks)),
@@ -406,7 +424,7 @@
             dma((chunks,)),
         ],
         compiler_params=pltpu.CompilerParams(
-            collective_id=0, has_side_effects=True, vmem_limit_bytes=48 * 2**20
+            collective_id=0, has_side_effects=True, vmem_limit_bytes=ROOM
         ),
         cost_estimate=pl.CostEstimate(
             flops=4 * slots * wide * features,
@@ -414,6 +432,14 @@
             transcendentals=0,
         ),
     )(gate_rows.T, route_rows.T, scales, gradient, activations, weight)
+    return pl.pallas_call(
+        store,
+        out_shape=shapes,
+        in_specs=[pl.BlockSpec(memory_space=pltpu.HBM)] * 2,
+        out_specs=(pl.BlockSpec(memory_space=pltpu.HBM),) * 2,
+        scratch_shapes=[dma((2,))],
+        compiler_params=pltpu.CompilerParams(vmem_limit_bytes=ROOM),
+    )(*results)
 
 
 def on_device(out_grad, gate_weights, routes, hidden_act, down_weight, block_scales):

time: 46.5 us -> 90.4 us (1.94)
  Pallas kernels: 39.9 us -> 89.6 us
  local copies, waits for them, and re-layouts: 5.67 us -> 0 us
    pallas_call x1 -> x2, Pallas kernels: 39.9 us -> 89.6 us  [the longest x1 48.8 us: every_expert(): pl.pallas_call(store, out_shape=shapes, in_specs=[pl.BlockSpec(memory_spa...]
    unnamed x14 -> x0, local copies, waits for them, and re-layouts: 5.67 us -> none
where the time goes in v2:
time: 90.4 us; the launch traced here: 90.2 us
  Pallas kernels  89.6 us (99%)
    pallas_call x1, Pallas kernels, every_expert(): pl.pallas_call(store, out_shape=shapes, in_specs=[pl.BlockSpec(memory_spa...  48.8 us
    pallas_call x1, Pallas kernels, every_expert(): pl.pallas_call(functools.partial(kernel, sections, experts), out_shape=sh...  40.8 us

profile of v2, /device:TPU:0, one launch (start us, length us, event | category | flops | bytes accessed | tf_op | source)
XLA Modules:
  0.0 90.2 jit_solution(1303820568897585900)
XLA Ops:
  0.6 40.8 %shard_map.77 = (bf16[1024,512]{1,0:T(8,128)(2,1)}, bf16[256,1024]{1,0:T(8,128)(2,1)}) custom-call(f32[8,128]{1,0:T(8,128)} %bitcast.17, s32[8,128]{1,0:T(8,128)} %bitcast.18, f32[2,8]{1,0:T(2,128)} %bitcast.19, bf16[128,1024]{1,0:T(8,128)(2,1)} %bitcast.16, bf16[1024,512]{1,0:T(8,128)(2,1)} %bitcast.12, bf16[256,1024]{1,0:T(8,128)(2,1)} %bitcast.14), custom_call_target="tpu_custom_call" | custom-call | flops 2147483648 | bytes 3670016 | tf_op jit(solution)/shard_map/pallas_call | solution.py:391
  41.4 48.8 %shard_map.78 = (bf16[1024,512]{1,0:T(8,128)(2,1)}, bf16[256,1024]{1,0:T(8,128)(2,1)}) custom-call(bf16[1024,512]{1,0:T(8,128)(2,1)} %get-tuple-element.6.hidden_ref, bf16[256,1024]{1,0:T(8,128)(2,1)} %get-tuple-element.7.grad_ref), custom_call_target="tpu_custom_call" | custom-call | tf_op jit(solution)/shard_map/pallas_call | solution.py:435

commit v3 on v2

--- a/solution.py
+++ b/solution.py
@@ -9,6 +9,7 @@
 
 QBLOCK = 128
 WIDTH = 256
+PIECES = 4
 ROOM = 63 * 2**20
 MESH = pl.DeviceIdType.MESH
 
@@ -107,7 +108,7 @@
     load_g = pltpu.make_async_copy(gates_hbm, gates_ref, load_sem.at[3])
     load_r = pltpu.make_async_copy(routes_hbm, routes_ref, load_sem.at[4])
     load_s = pltpu.make_async_copy(scales_hbm, scales_ref, load_sem.at[5])
-    for load in (load_x, load_w, load_s, load_g, load_r, load_a):
+    for load in (load_g, load_r, load_x, load_s, load_w, load_a):
         load.start()
 
     barrier = pltpu.get_barrier_semaphore()
@@ -116,6 +117,13 @@
         pl.semaphore_signal(barrier, inc=1, device_id=(section, peer), device_id_type=MESH)
     pl.semaphore_signal(barrier, inc=1, device_id=(pair, me), device_id_type=MESH)
 
+    load_g.wait()
+    load_r.wait()
+    for expert in range(experts):
+        gate_out[expert] = jnp.sum(
+            jnp.where(routes_ref[...] == expert, gates_ref[...], 0.0), axis=0, keepdims=True
+        )
+    gate_in[me] = gate_out[me]
     load_x.wait()
     pl.semaphore_wait(barrier, experts)
 
@@ -172,6 +180,8 @@
             device_id_type=MESH,
         )
 
+    for step in range(1, experts):
+        gate_copy(lax.rem(me + step, experts), me).start()
     send_own(0)
     send_own(1)
 
@@ -191,16 +201,6 @@
                 ] = (piece.astype(jnp.float32) * scales_ref[row, column]).astype(jnp.bfloat16)
         weight_copy(chunk, upper).start()
 
-    load_g.wait()
-    load_r.wait()
-    for expert in range(experts):
-        gate_out[expert] = jnp.sum(
-            jnp.where(routes_ref[...] == expert, gates_ref[...], 0.0), axis=0, keepdims=True
-        )
-    gate_in[me] = gate_out[me]
-    for step in range(1, experts):
-        gate_copy(lax.rem(me + step, experts), me).start()
-
     load_a.wait()
 
     @pl.loop(0, slots // WIDTH)
@@ -365,15 +365,22 @@
     store_g.wait()
 
 
-def store(hidden_ref, grad_ref, hidden_hbm, grad_hbm, sem):
-    copies = [
-        pltpu.make_async_copy(hidden_ref, hidden_hbm, sem.at[0]),
-        pltpu.make_async_copy(grad_ref, grad_hbm, sem.at[1]),
-    ]
-    for copy in copies:
-        copy.start()
-    for copy in copies:
-        copy.wait()
+def store(hidden_hbm, grad_hbm, hidden_out, grad_out, hidden_ref, grad_ref, in_sem, out_sem):
+    ways = ((hidden_hbm, hidden_ref, hidden_out), (grad_hbm, grad_ref, grad_out))
+    loads, stores = [], []
+    for source, held, target in ways:
+        rows = source.shape[0] // PIECES
+        for piece in range(PIECES):
+            at, place = pl.ds(piece * rows, rows), len(loads)
+            loads.append(pltpu.make_async_copy(source.at[at], held.at[at], in_sem.at[place]))
+            stores.append(pltpu.make_async_copy(held.at[at], target.at[at], out_sem.at[place]))
+    for load in loads:
+        load.start()
+    for load, put in zip(loads, stores):
+        load.wait()
+        put.start()
+    for put in stores:
+        put.wait()
 
 
 def every_expert(gradient, gate_rows, route_rows, activations, weight, scales):
@@ -437,7 +444,12 @@
         out_shape=shapes,
         in_specs=[pl.BlockSpec(memory_space=pltpu.HBM)] * 2,
         out_specs=(pl.BlockSpec(memory_space=pltpu.HBM),) * 2,
-        scratch_shapes=[dma((2,))],
+        scratch_shapes=[
+            pltpu.VMEM((slots, wide), bf16),
+            pltpu.VMEM((half, features), bf16),
+            dma((2 * PIECES,)),
+            dma((2 * PIECES,)),
+        ],
         compiler_params=pltpu.CompilerParams(vmem_limit_bytes=ROOM),
     )(*results)
 

time: 90.4 us -> 42.9 us (0.47)
  Pallas kernels: 89.6 us -> 42.1 us
    pallas_call x1, Pallas kernels: 48.8 us -> 2.22 us  [every_expert(): pl.pallas_call(store, out_shape=shapes, in_specs=[pl.BlockSpec(memory_spa...]
    pallas_call x1, Pallas kernels: 40.8 us -> 39.9 us  [every_expert(): pl.pallas_call(functools.partial(kernel, sections, experts), out_shape=sh...]
where the time goes in v3:
time: 42.9 us; the launch traced here: 42.7 us
  Pallas kernels  42.1 us (98%)
  between operations  0.64 us (1%)
    pallas_call x1, Pallas kernels, every_expert(): pl.pallas_call(functools.partial(kernel, sections, experts), out_shape=sh...  39.9 us
    pallas_call x1, Pallas kernels, every_expert(): pl.pallas_call(store, out_shape=shapes, in_specs=[pl.BlockSpec(memory_spa...  2.22 us

profile of v3, /device:TPU:0, one launch (start us, length us, event | category | flops | bytes accessed | tf_op | source)
XLA Modules:
  0.0 42.7 jit_solution(17964724163253441925)
XLA Ops:
  0.6 39.9 %shard_map.77 = (bf16[1024,512]{1,0:T(8,128)(2,1)}, bf16[256,1024]{1,0:T(8,128)(2,1)}) custom-call(f32[8,128]{1,0:T(8,128)} %bitcast.17, s32[8,128]{1,0:T(8,128)} %bitcast.18, f32[2,8]{1,0:T(2,128)} %bitcast.19, bf16[128,1024]{1,0:T(8,128)(2,1)} %bitcast.16, bf16[1024,512]{1,0:T(8,128)(2,1)} %bitcast.12, bf16[256,1024]{1,0:T(8,128)(2,1)} %bitcast.14), custom_call_target="tpu_custom_call" | custom-call | flops 2147483648 | bytes 3670016 | tf_op jit(solution)/shard_map/pallas_call | solution.py:398
  40.5 2.2 %shard_map.78 = (bf16[1024,512]{1,0:T(8,128)(2,1)}, bf16[256,1024]{1,0:T(8,128)(2,1)}) custom-call(bf16[1024,512]{1,0:T(8,128)(2,1)} %get-tuple-element.6.hidden_hbm, bf16[256,1024]{1,0:T(8,128)(2,1)} %get-tuple-element.7.grad_hbm), custom_call_target="tpu_custom_call" | custom-call | tf_op jit(solution)/shard_map/pallas_call | solution.py:442

commit v4 on v3

--- a/solution.py
+++ b/solution.py
@@ -8,7 +8,8 @@
 from jax.sharding import PartitionSpec as P
 
 QBLOCK = 128
-WIDTH = 256
+WIDTH = 512
+TILE = 256
 PIECES = 4
 ROOM = 63 * 2**20
 MESH = pl.DeviceIdType.MESH
@@ -203,9 +204,9 @@
 
     load_a.wait()
 
-    @pl.loop(0, slots // WIDTH)
+    @pl.loop(0, slots // TILE)
     def _(tile):
-        at = pl.ds(pl.multiple_of(tile * WIDTH, WIDTH), WIDTH)
+        at = pl.ds(pl.multiple_of(tile * TILE, TILE), TILE)
         act_t[:, at] = act[at, :].T
 
     for step in range(1, experts):
@@ -298,9 +299,9 @@
     for chunk in range(chunks):
         weight_copy(chunk, 1 - upper).wait_recv()
 
-    @pl.loop(0, slots // WIDTH)
+    @pl.loop(0, slots // TILE)
     def _(tile):
-        at = pl.ds(pl.multiple_of(tile * WIDTH, WIDTH), WIDTH)
+        at = pl.ds(pl.multiple_of(tile * TILE, TILE), TILE)
         total = None
         for chunk in range(chunks):
             term = lax.dot_general(

time: 42.9 us -> 41.2 us (0.960)
  Pallas kernels: 42.1 us -> 40.3 us
    pallas_call x1, Pallas kernels: 39.9 us -> 38.1 us  [every_expert(): pl.pallas_call(functools.partial(kernel, sections, experts), out_shape=sh...]
where the time goes in v4:
time: 41.2 us; the launch traced here: 41 us
  Pallas kernels  40.3 us (98%)
  between operations  0.64 us (2%)
    pallas_call x1, Pallas kernels, every_expert(): pl.pallas_call(functools.partial(kernel, sections, experts), out_shape=sh...  38.1 us
    pallas_call x1, Pallas kernels, every_expert(): pl.pallas_call(store, out_shape=shapes, in_specs=[pl.BlockSpec(memory_spa...  2.22 us

profile of v4, /device:TPU:0, one launch (start us, length us, event | category | flops | bytes accessed | tf_op | source)
XLA Modules:
  0.0 41.0 jit_solution(10491477482608721283)
XLA Ops:
  0.6 38.1 %shard_map.77 = (bf16[1024,512]{1,0:T(8,128)(2,1)}, bf16[256,1024]{1,0:T(8,128)(2,1)}) custom-call(f32[8,128]{1,0:T(8,128)} %bitcast.17, s32[8,128]{1,0:T(8,128)} %bitcast.18, f32[2,8]{1,0:T(2,128)} %bitcast.19, bf16[128,1024]{1,0:T(8,128)(2,1)} %bitcast.16, bf16[1024,512]{1,0:T(8,128)(2,1)} %bitcast.12, bf16[256,1024]{1,0:T(8,128)(2,1)} %bitcast.14), custom_call_target="tpu_custom_call" | custom-call | flops 2147483648 | bytes 3670016 | tf_op jit(solution)/shard_map/pallas_call | solution.py:399
  38.8 2.2 %shard_map.78 = (bf16[1024,512]{1,0:T(8,128)(2,1)}, bf16[256,1024]{1,0:T(8,128)(2,1)}) custom-call(bf16[1024,512]{1,0:T(8,128)(2,1)} %get-tuple-element.6.hidden_hbm, bf16[256,1024]{1,0:T(8,128)(2,1)} %get-tuple-element.7.grad_hbm), custom_call_target="tpu_custom_call" | custom-call | tf_op jit(solution)/shard_map/pallas_call | solution.py:443
